TPU v7x, 256 devices: a whole 4x4x8 slice. The times are simulated.
256 devices in a mesh: pair: 64 (over y, x_hi, z), aux: 4 (over x_lo, core).
Axes of the slice: x: 4 (x_hi: 2, x_lo: 2; x = x_hi * 2 + x_lo), y: 4, z: 8, core: 2. Of those that a mesh axis runs over, the one named last changes fastest.
Arguments:
- x_panels: float32 [1024, 8192], P(None, 'pair'), may hold values from -0.1875 to 0.1875
- xbar_panels: float32 [1024, 8192], P(None, 'pair'), may hold values from -6 to 6
- bbar_below: float32 [4096, 8192], P('aux', 'pair'), may hold values from -16 to 16
- l_below: float32 [4096, 1024], P(('aux', 'pair')), may hold values from -0.09375 to 0.09375
- l_cross: float32 [512, 512], P('pair'), may hold values from -0.25 to 0.25
- dinv: float32 [2, 512, 512], P(None, 'pair'), as said below
Outputs:
- bbar_panels: float32 [1024, 8192], P(None, 'pair')
- lbar_below: float32 [4096, 1024], P(('aux', 'pair'))
- lbar_diag: float32 [2, 512, 512], P(None, 'pair')
- lbar_cross: float32 [512, 512], P('pair')
Inputs may be any that keep to these rules, and one draw needn't show every extreme that they name: Each dinv[k] is lower triangular with a positive diagonal.
All inputs are finite; a program needn't handle non-finite values.
Results may differ from a plain program's by a relative error of at most 0.00013.
Values sent between devices are 32-bit elements; how exact they have to be, the bound alone decides.
A program may use at most 64 MiB of HBM per device.

v0:
```python
import jax
import jax.numpy as jnp
from jax import lax
from jax.sharding import PartitionSpec as P


def fold_with(right_side, pieces):
    return lax.dot_general(
        pieces,
        right_side,
        (((0,), (0,)), ((), ())),
        precision=lax.Precision.HIGHEST,
        preferred_element_type=jnp.float32,
    )


def body(x_panels, xbar_panels, bbar_below, l_below, l_cross, dinv):
    panel = dinv.shape[2]
    precise = lax.Precision.HIGHEST
    contract_cols = (((1,), (1,)), ((), ()))

    def below_correction(first, count):
        columns = l_below[:, first : first + count]
        folded = fold_with(bbar_below, lax.all_gather(columns, "pair", axis=0, tiled=True))
        return lax.psum(folded, "aux")

    def factor_terms(first, count):
        x_rows = x_panels[first : first + count]
        return lax.psum_scatter(
            -lax.dot_general(
                bbar_below,
                x_rows,
                contract_cols,
                precision=precise,
                preferred_element_type=jnp.float32,
            ),
            "pair",
            scatter_dimension=0,
            tiled=True,
        )

    def solve_panel(index, right_side):
        return fold_with(right_side, lax.all_gather(dinv[index], "pair", axis=0, tiled=True))

    late_corr = below_correction(panel, panel)
    bbar_late = solve_panel(1, xbar_panels[panel:] - late_corr)
    late_factor = factor_terms(panel, panel)
    cross_term = fold_with(bbar_late, lax.all_gather(l_cross, "pair", axis=0, tiled=True))
    early_corr = below_correction(0, panel)
    bbar_early = solve_panel(0, xbar_panels[:panel] - early_corr - cross_term)
    early_factor = factor_terms(0, panel)
    lbar_below = jnp.concatenate([early_factor, late_factor], axis=1)
    x_early = x_panels[:panel]
    x_late = x_panels[panel:]
    diag_early = -lax.dot_general(
        bbar_early, x_early, contract_cols, precision=precise, preferred_element_type=jnp.float32
    )
    diag_late = -lax.dot_general(
        bbar_late, x_late, contract_cols, precision=precise, preferred_element_type=jnp.float32
    )
    cross_block = -lax.dot_general(
        bbar_late, x_early, contract_cols, precision=precise, preferred_element_type=jnp.float32
    )
    stacked = jnp.stack([diag_early, diag_late, cross_block])
    summed = lax.psum_scatter(stacked, "pair", scatter_dimension=1, tiled=True)
    bbar_panels = jnp.concatenate([bbar_early, bbar_late], axis=0)
    return (bbar_panels, lbar_below, summed[:2], summed[2])


def solution(mesh):
    in_specs = (
        P(None, "pair"),
        P(None, "pair"),
        P("aux", "pair"),
        P(("aux", "pair"), None),
        P("pair", None),
        P(None, "pair", None),
    )
    out_specs = (P(None, "pair"), P(("aux", "pair"), None), P(None, "pair", None), P("pair", None))
    return jax.shard_map(body, mesh=mesh, in_specs=in_specs, out_specs=out_specs, check_vma=False)
```

profile of v0, /device:TPU:2, one launch (start us, length us, event | category | flops | bytes accessed | tf_op | source)
XLA Modules:
  0.0 1741.1 jit_solution(4835709447425848421)
XLA Ops:
  7.2 0.0 copy-start
  7.2 0.0 all-gather.8.cloned.1.call-start
  7.2 1.5 fusion.15
  8.7 0.0 all-gather.8.cloned.1.call-update
  8.7 0.0 all-gather.10.cloned.1.call-start
  8.8 0.7 all-gather.10.cloned.1.call-update
  9.5 0.0 all-gather.14.cloned.1.call-start
  9.5 1.3 fusion.16
  10.8 0.0 all-gather.14.cloned.1.call-update
  10.9 0.0 all-reduce.3.cloned.1.call-start
  10.9 122.0 %all-gather.8.cloned.1.call-done = f32[1024,512]{1,0:T(8,128)} async-done(((f32[16,512]{1,0:T(8,128)}), f32[1024,512]{1,0:T(8,128)}) %all-gather.8.cloned.1.call-update) | async-done | bytes 2097168 | tf_op jit(solution)/shard_map/all_gather | solution.py:24
  132.9 0.0 copy-done
  132.9 5.7 fusion.17
  138.6 0.0 copy-start.1
  138.6 113.9 %all-gather.10.cloned.1.call-done = f32[1024,512]{1,0:T(8,128)} async-done(((f32[16,512]{1,0:T(8,128)}), f32[1024,512]{1,0:T(8,128)}) %all-gather.10.cloned.1.call-update) | async-done | bytes 2097168 | tf_op jit(solution)/shard_map/all_gather | solution.py:24
  252.5 5.7 fusion.18
  258.2 0.0 all-reduce.3.cloned.1.call-update
  258.3 0.0 all-gather.12.cloned.1.call-start
  258.3 0.5 all-gather.12.cloned.1.call-update
  258.9 0.0 all-gather.16.cloned.1.call-start
  258.9 0.5 all-gather.16.cloned.1.call-update
  259.4 0.0 reduce-scatter.6.cloned.1.call-start
  259.5 0.0 copy-done.1
  259.5 3.1 convolution_negate_fusion
  262.6 0.0 reduce-scatter.6.cloned.1.call-update
  262.6 0.0 copy-start.4
  262.6 0.0 reduce-scatter.4.cloned.1.call-start
  262.7 3.2 convolution_negate_fusion.1
  265.8 0.0 reduce-scatter.4.cloned.1.call-update
  265.8 0.2 reduce-scatter.8.cloned.1.call-start
  266.1 101.1 %all-gather.14.cloned.1.call-done = f32[1,512,512]{2,1,0:T(8,128)} async-done(((f32[1,8,512]{2,1,0:T(8,128)}), f32[1,512,512]{2,1,0:T(8,128)}) %all-gather.14.cloned.1.call-update) | async-done | bytes 1048592 | tf_op jit(solution)/shard_map/all_gather | solution.py:43
  367.2 43.0 %all-reduce.3.cloned.1.call-done = (f32[512,128]{1,0:T(8,128)}, f32[512,128]{1,0:T(8,128)}) async-done(((f32[512,128]{1,0:T(8,128)}, f32[512,128]{1,0:T(8,128)}), (f32[512,128]{1,0:T(8,128)}, f32[512,128]{1,0:T(8,128)})) %all-reduce.3.cloned.1.call-update) | async-done | bytes 524304 | tf_op jit(solution)/shard_map/psum | solution.py:25
  410.3 0.0 copy-done.4
  410.3 2.1 fusion.6
  412.4 1.0 fusion
  413.4 1.0 fusion.1
  414.4 114.3 %all-gather.12.cloned.1.call-done = f32[512,512]{1,0:T(8,128)} async-done(((f32[8,512]{1,0:T(8,128)}), f32[512,512]{1,0:T(8,128)}) %all-gather.12.cloned.1.call-update) | async-done | bytes 1048592 | tf_op jit(solution)/shard_map/all_gather | solution.py:48
  528.7 3.9 fusion.3
  532.5 111.3 %all-gather.16.cloned.1.call-done = f32[1,512,512]{2,1,0:T(8,128)} async-done(((f32[1,8,512]{2,1,0:T(8,128)}), f32[1,512,512]{2,1,0:T(8,128)}) %all-gather.16.cloned.1.call-update) | async-done | bytes 1048592 | tf_op jit(solution)/shard_map/all_gather | solution.py:43
  643.9 2.1 fusion.4
  645.9 0.0 copy-start.2
  645.9 0.7 copy-done.2
  646.6 1.0 fusion.2
  647.7 2.0 pad_maximum_fusion
  649.7 0.0 copy-start.3
  649.7 0.0 reduce-scatter.8.cloned.1.call-update
  649.7 359.2 %reduce-scatter.6.cloned.1.call-done = f32[16,512]{1,0:T(8,128)} async-done(((f32[1024,512]{1,0:T(8,128)}), f32[16,512]{1,0:T(8,128)}) %reduce-scatter.6.cloned.1.call-update) | async-done | bytes 32784 | tf_op jit(solution)/shard_map/reduce_scatter | solution.py:29
  1008.9 360.5 %reduce-scatter.4.cloned.1.call-done = f32[16,512]{1,0:T(8,128)} async-done(((f32[1024,512]{1,0:T(8,128)}), f32[16,512]{1,0:T(8,128)}) %reduce-scatter.4.cloned.1.call-update) | async-done | bytes 32784 | tf_op jit(solution)/shard_map/reduce_scatter | solution.py:29
  1369.4 1.4 pad_maximum_fusion.2
  1370.8 0.0 copy-done.3
  1370.8 1.0 copy.10
  1371.8 360.0 %reduce-scatter.8.cloned.1.call-done = f32[3,8,512]{2,1,0:T(8,128)} async-done(((f32[3,512,512]{2,1,0:T(8,128)}), f32[3,8,512]{2,1,0:T(8,128)}) %reduce-scatter.8.cloned.1.call-update) | async-done | bytes 49168 | tf_op jit(solution)/shard_map/reduce_scatter | solution.py:65
  1731.8 1.3 slice_bitcast_fusion
  1733.2 1.4 slice.42
  (1 shorter events, 0.0 us)
Async XLA Ops:
  7.2 125.7 %copy-start = (f32[1024,128]{1,0:T(8,128)S(1)}, f32[1024,128]{1,0:T(8,128)}, u32[]{:S(2)}) copy-start(f32[1024,128]{1,0:T(8,128)} %param.8) | copy-start | bytes 1572868
  7.2 125.7 %all-gather.8.cloned.1.call-start = ((), (), s32[]{:S(2)}) async-start(), calls=%async_computation.3 | async-start | bytes 2129920 | tf_op jit(solution)/shard_map/all_gather | solution.py:24
  8.7 243.8 %all-gather.10.cloned.1.call-start = ((), (), s32[]{:S(2)}) async-start(), calls=%async_computation.4 | async-start | bytes 2129920 | tf_op jit(solution)/shard_map/all_gather | solution.py:24
  9.5 357.8 %all-gather.14.cloned.1.call-start = ((), (), s32[]{:S(2)}) async-start(), calls=%async_computation.9 | async-start | bytes 1064960 | tf_op jit(solution)/shard_map/all_gather | solution.py:43
  10.9 399.4 %all-reduce.3.cloned.1.call-start = ((), (), s32[]{:S(2)}) async-start(), calls=%async_computation.11 | async-start | bytes 1048576 | tf_op jit(solution)/shard_map/psum | solution.py:25
  138.6 120.9 %copy-start.1 = (f32[1024,128]{1,0:T(8,128)S(1)}, f32[1024,128]{1,0:T(8,128)}, u32[]{:S(2)}) copy-start(f32[1024,128]{1,0:T(8,128)} %param.6) | copy-start | bytes 1572868
  258.3 270.4 %all-gather.12.cloned.1.call-start = ((), (), s32[]{:S(2)}) async-start(), calls=%async_computation.5 | async-start | bytes 1064960 | tf_op jit(solution)/shard_map/all_gather | solution.py:48
  258.9 385.0 %all-gather.16.cloned.1.call-start = ((), (), s32[]{:S(2)}) async-start(), calls=%async_computation.10 | async-start | bytes 1064960 | tf_op jit(solution)/shard_map/all_gather | solution.py:43
  259.4 749.5 %reduce-scatter.6.cloned.1.call-start = ((), (), s32[]{:S(2)}) async-start(), calls=%async_computation.7 | async-start | bytes 2129920 | tf_op jit(solution)/shard_map/reduce_scatter | solution.py:29
  262.6 147.7 %copy-start.4 = (f32[1024,128]{1,0:T(8,128)S(1)}, f32[1024,128]{1,0:T(8,128)}, u32[]{:S(2)}) copy-start(f32[1024,128]{1,0:T(8,128)} %param.7) | copy-start | bytes 1572868
  262.6 1106.7 %reduce-scatter.4.cloned.1.call-start = ((), (), s32[]{:S(2)}) async-start(), calls=%async_computation.6 | async-start | bytes 2129920 | tf_op jit(solution)/shard_map/reduce_scatter | solution.py:29
  265.8 1466.0 %reduce-scatter.8.cloned.1.call-start = ((), (), s32[]{:S(2)}) async-start(), calls=%async_computation.8 | async-start | bytes 3194880 | tf_op jit(solution)/shard_map/reduce_scatter | solution.py:65
  645.9 0.7 copy-start.2
  649.7 721.1 %copy-start.3 = (f32[128,512]{1,0:T(8,128)S(1)}, f32[128,512]{1,0:T(8,128)}, u32[]{:S(2)}) copy-start(f32[128,512]{1,0:T(8,128)} %copy-done.2) | copy-start | bytes 786436
Sparse Core Ops, SparseCore 0:
  12.2 120.6 all-gather.7
  137.0 115.4 all-gather.9
  256.2 111.0 all-gather.13
  370.3 39.8 all-reduce.2
  413.7 114.8 all-gather.11
  532.8 111.0 all-gather.15
  646.4 362.4 reduce-scatter.5
  1011.5 357.7 reduce-scatter.3
  1371.9 359.9 reduce-scatter.7
where the time goes:
time: 1740 us
  waiting for transfers between devices  1690 us (97%)
  matrix products  28.8 us (2%)
    reduce_scatter x2, waiting for transfers between devices, factor_terms(): lax.psum_scatter(-lax.dot_general(bbar_below, x_rows, contract_cols, prec...  720 us
    reduce_scatter x1, waiting for transfers between devices, body(): summed = lax.psum_scatter(stacked, 'pair', scatter_dimension=1, tiled=True)  360 us
    all_gather x2, waiting for transfers between devices, below_correction(): lax.all_gather(columns, 'pair', axis=0, tiled=True)  236 us
    all_gather x2, waiting for transfers between devices, solve_panel(): lax.all_gather(dinv[index], 'pair', axis=0, tiled=True)  212 us
    all_gather x1, waiting for transfers between devices, body(): lax.all_gather(l_cross, 'pair', axis=0, tiled=True)  114 us
    psum x1, waiting for transfers between devices, below_correction(): return lax.psum(folded, 'aux')  43 us
  transfers between devices with their start and end apart: 9, of which 9 were waited for; matrix products, arithmetic and copies ran while one was open for 2% of the time, Pallas kernels for 0%

commit v1 on v0

v1 whole, which is shorter than its diff:
```python
import jax
import jax.numpy as jnp
from jax import lax
from jax.experimental import pallas as pl
from jax.experimental.pallas import tpu as pltpu
from jax.sharding import PartitionSpec as P

MESH = pl.DeviceIdType.MESH
F32 = jnp.float32
BF16 = jnp.bfloat16
NN = ((1,), (0,))
NT = ((1,), (1,))

L_Z, L_H, B_Y, G_Z, G_Y, G_H, X_Y, X_C = 0, 8, 16, 20, 28, 32, 36, 40
R_C, R_Y, R_L, S_C, D_Y, C_Y, D_H, D_Z, D_A, F_Z, F_H = (
    44, 46, 54, 56, 60, 64, 68, 70, 78, 82, 90)
COPIES = 92

Z_ORDER = (1, 7, 2, 6, 3, 5, 4)


def halves(value):
    high = value.astype(BF16)
    return high, (value - high.astype(F32)).astype(BF16)


def dot3(a, b, dims):
    def one(s, t):
        return lax.dot_general(s, t, (dims, ((), ())), preferred_element_type=F32)

    return one(a[0], b[0]) + (one(a[0], b[1]) + one(a[1], b[0]))


def kernel(
    x_ref, xbar_ref, bbar_ref, l_ref, lc_ref, dinv_ref,
    panels_ref, lbelow_ref, ldiag_ref, lcross_ref,
    lg, lh, ll, gs, gh, gl, bb, bh, bl, th, tl, xx, xh, xl, xbt,
    cks, csend, crv, yr, accs, accr, lt, et, ch,
    dd, ddr, dc, dcr, ds, dhr, ez, ezr, fin, pp, zr, ps, hr,
    ss, rs,
):
    pair = lax.axis_index("pair")
    aux = lax.axis_index("aux")
    y, h, z = pair // 16, (pair // 8) % 2, pair % 8
    lo, core = aux // 2, aux % 2

    def at(dy=0, dh=0, dz=0, dl=0, dcore=0):
        place = ((y + dy) % 4 * 2 + (h + dh) % 2) * 8 + (z + dz) % 8
        return (place, (lo + dl) % 2 * 2 + (core + dcore) % 2)

    started = []

    def send(src, dst, place, to):
        copy = pltpu.make_async_remote_copy(
            src_ref=src, dst_ref=dst, send_sem=ss.at[place], recv_sem=rs.at[place],
            device_id=to, device_id_type=MESH)
        copy.start()
        return copy

    def keep(src, dst, place, to):
        copy = send(src, dst, place, to)
        started.append(copy)
        return copy

    lg[h, z] = l_ref[...]
    gs[y, h, z, :, 0:512] = jnp.where(core == 0, dinv_ref[0], dinv_ref[1])
    gs[y, h, z, :, 512:768] = jnp.where(core == 0, lc_ref[:, 0:256], lc_ref[:, 256:512])

    barrier = pltpu.get_barrier_semaphore()
    partners = [at(dy=d) for d in (1, 2, 3)] + [at(dz=k) for k in range(1, 8)]
    partners += [at(dh=1), at(dl=1), at(dcore=1), at(dl=1, dcore=1)]
    for partner in partners:
        pl.semaphore_signal(barrier, inc=1, device_id=partner, device_id_type=MESH)
    pl.semaphore_wait(barrier, len(partners))

    mine = lg.at[h, z]
    l_z = {k: keep(mine, mine, L_Z + k, at(dz=k)) for k in Z_ORDER}
    l_h = {0: keep(mine, mine, L_H, at(dh=1))}
    b_y = {}
    for d in (2, 1, 3):
        rows = pl.ds((y + d) % 4 * 256, 256)
        b_y[d] = keep(bbar_ref.at[rows], bb.at[d - 1], B_Y + d, at(dy=d))
    mine = gs.at[y, h, z]
    g_z = {k: keep(mine, mine, G_Z + k, at(dz=k)) for k in Z_ORDER}

    def take_b(d, value):
        cols = slice(d * 128, (d + 1) * 128)
        high, low = halves(value)
        bh[:, cols] = high
        bl[:, cols] = low
        high, low = halves(value.T)
        th[cols, :] = high
        tl[cols, :] = low

    take_b(0, bbar_ref[pl.ds(y * 256, 256), :])

    def l_forward(k):
        l_z[k].wait_recv()
        block = lg.at[h, (z + 8 - k) % 8]
        l_h[k] = keep(block, block, L_H + k, at(dh=1))

    l_forward(1)
    l_forward(7)
    xbt[...] = xbar_ref[pl.ds(core * 512, 512), :].T
    l_forward(2)
    l_forward(6)
    for d in (1, 3):
        b_y[d].wait_recv()
        take_b(d, bb[d - 1])
    l_forward(3)
    l_forward(5)
    l_forward(4)
    b_y[2].wait_recv()
    take_b(2, bb[1])

    for k in Z_ORDER:
        g_z[k].wait_recv()
    mine = gs.at[y, h]
    g_y = {d: keep(mine, mine, G_Y + d, at(dy=d)) for d in (1, 3, 2)}
    g_h = {0: keep(mine, mine, G_H, at(dh=1))}

    half = x_ref.at[pl.ds(core * 512, 512)]
    x_y = {d: keep(half, xx.at[d - 1, core], X_Y + d, at(dy=d)) for d in (1, 3, 2)}
    high, low = halves(x_ref[...])
    xh[:, 0:128] = high
    xl[:, 0:128] = low

    for k in (0,) + Z_ORDER:
        l_h[k].wait_recv()
    for part in range(2):
        high, low = halves(lg[:, :, :, part * 512 : (part + 1) * 512].reshape(256, 512))
        lh[part] = high
        ll[part] = low

    turned = (th[...], tl[...])
    r_c = []
    for q in range(2):
        cols = slice(q * 256, (q + 1) * 256)
        other = (lh[1 - core, :, cols], ll[1 - core, :, cols])
        csend[q] = dot3(turned, other, NN).reshape(4, 128, 256)
        r_c.append(keep(csend.at[q], crv.at[q], R_C + q, at(dcore=1)))
        own = (lh[core, :, cols], ll[core, :, cols])
        cks[q] = dot3(turned, own, NN).reshape(4, 128, 256)
    r_y = {}
    for q in range(2):
        r_c[q].wait_recv()
        for d in (2, 1, 3, 0):
            cks[q, d] += crv[q, d]
            if d:
                r_y[q, d] = keep(cks.at[q, d], yr.at[q, d - 1], R_Y + 4 * q + d, at(dy=4 - d))

    for d in (1, 3, 2):
        g_y[d].wait_recv()
        block = gs.at[(y + 4 - d) % 4, h]
        g_h[d] = keep(block, block, G_H + d, at(dh=1))

    r_l = []
    for q in range(2):
        for d in (1, 3, 2):
            r_y[q, d].wait_recv()
        accs[q] = (cks[q, 0] + yr[q, 0]) + (yr[q, 1] + yr[q, 2])
        r_l.append(keep(accs.at[q], accr.at[q], R_L + q, at(dl=1)))

    x_c = {}
    for d in (1, 3, 2):
        x_y[d].wait_recv()
        block = xx.at[d - 1, core]
        x_c[d] = keep(block, block, X_C + d, at(dcore=1))
    for d in (1, 3, 2):
        x_c[d].wait_recv()
        cols = slice(d * 128, (d + 1) * 128)
        high, low = halves(xx[d - 1].reshape(1024, 128))
        xh[:, cols] = high
        xl[:, cols] = low
    for part in range(4):
        rows = slice(part * 256, (part + 1) * 256)
        product = dot3((bh[...], bl[...]), (xh[rows, :], xl[rows, :]), NT)
        pp[:, :, :, rows] = product.reshape(2, 8, 16, 256)
    f_z = {k: keep(pp.at[:, (z + k) % 8], zr.at[k - 1], F_Z + k, at(dz=k)) for k in Z_ORDER}

    for d in (0, 1, 3, 2):
        g_h[d].wait_recv()
    high, low = halves(gs[...].reshape(512, 768))
    gh[...] = high
    gl[...] = low
    for q in range(2):
        r_l[q].wait_recv()

    def x_rows(start, count):
        rows = pl.ds(pl.multiple_of(start, 128), count)
        return xh[rows, 0:128], xl[rows, 0:128]

    def block_of(columns):
        return gh[:, columns], gl[:, columns]

    solve_cols, cross_cols = slice(0, 512), slice(512, 768)
    to_core = at(dcore=1)

    def copy_of(ref, place):
        return pltpu.make_async_remote_copy(
            src_ref=ref, dst_ref=ref, send_sem=ss.at[place], recv_sem=rs.at[place],
            device_id=to_core, device_id_type=MESH)

    def corrected():
        return xbt[...] - jnp.concatenate([accs[0] + accr[0], accs[1] + accr[1]], axis=1)

    def diag_product(turned_rows):
        rows = turned_rows.T
        product = dot3(halves(rows), x_rows(core * 512 + lo * 256, 256), NT)
        dd[...] = product.reshape(4, 128, 256)
        return rows

    @pl.when(core == 1)
    def _():
        late = dot3(halves(corrected()), block_of(solve_cols), NN)
        lt[...] = late
        copy_of(lt, S_C).start()
        ch[...] = dot3(halves(late), block_of(cross_cols), NN)
        copy_of(ch, S_C + 1).start()
        panels_ref[512:1024, :] = diag_product(late)

    @pl.when(core == 0)
    def _():
        rest = corrected()
        copy_of(lt, S_C).wait_recv()
        cross = dot3(halves(lt[...]), block_of(cross_cols), NN)
        copy_of(ch, S_C + 1).wait_recv()
        rest = rest - jnp.concatenate([cross, ch[...]], axis=1)
        early = dot3(halves(rest), block_of(solve_cols), NN)
        et[...] = early
        copy_of(et, S_C + 2).start()
        panels_ref[0:512, :] = diag_product(early)

    d_y = {}
    for d in (2, 1, 3):
        d_y[d] = keep(dd.at[(y + d) % 4], ddr.at[d - 1], D_Y + d, at(dy=d))
    late = lt[...].T
    product = dot3(halves(late), x_rows(aux * 128, 128), NT)
    dc[...] = product.reshape(4, 128, 128)
    c_y = {}
    for d in (2, 1, 3):
        c_y[d] = keep(dc.at[(y + d) % 4], dcr.at[d - 1], C_Y + d, at(dy=d))

    @pl.when(core == 0)
    def _():
        panels_ref[512:1024, :] = late

    for k in Z_ORDER:
        f_z[k].wait_recv()
    total = pp[:, z]
    for k in range(7):
        total = total + zr[k]
    ps[...] = total
    f_h = keep(ps.at[1 - h], hr, F_H, at(dh=1))

    for d in (1, 3, 2):
        d_y[d].wait_recv()
        c_y[d].wait_recv()
    total = (dd[y] + ddr[0]) + (ddr[1] + ddr[2])
    ds[:, :, :, 0:256] = total.reshape(2, 8, 8, 256)
    total = (dc[y] + dcr[0]) + (dcr[1] + dcr[2])
    ds[:, :, :, 256:384] = total.reshape(2, 8, 8, 128)
    d_h = keep(ds.at[1 - h], dhr, D_H, at(dh=1))

    f_h.wait_recv()
    lbelow_ref[...] = -(ps[h] + hr[...])

    @pl.when(core == 1)
    def _():
        copy_of(et, S_C + 2).wait_recv()
        panels_ref[0:512, :] = et[...].T
        copy_of(lt, S_C).wait_send()
        copy_of(ch, S_C + 1).wait_send()

    @pl.when(core == 0)
    def _():
        copy_of(et, S_C + 2).wait_send()

    d_h.wait_recv()
    ez[...] = ds[h] + dhr[...]
    d_z = {k: keep(ez.at[(z + k) % 8], ezr.at[k - 1], D_Z + k, at(dz=k)) for k in Z_ORDER}
    for k in Z_ORDER:
        d_z[k].wait_recv()
    total = ez[z]
    for k in range(7):
        total = total + ezr[k]
    fin[aux] = -total
    d_a = []
    for j in (1, 2, 3):
        block = fin.at[aux]
        d_a.append(keep(block, block, D_A + j, at(dl=j // 2, dcore=j % 2)))
    for copy in d_a:
        copy.wait_recv()
    for part in range(4):
        which, side = part % 2, part // 2
        ldiag_ref[which, :, side * 256 : (side + 1) * 256] = fin[part, :, 0:256]
        lcross_ref[:, part * 128 : (part + 1) * 128] = fin[part, :, 256:384]

    for copy in started:
        copy.wait_send()


def body(x_panels, xbar_panels, bbar_below, l_below, l_cross, dinv):
    def vmem(*shape, dtype=F32):
        return pltpu.VMEM(shape, dtype)

    outs = (
        jax.ShapeDtypeStruct((1024, 128), F32),
        jax.ShapeDtypeStruct((16, 1024), F32),
        jax.ShapeDtypeStruct((2, 8, 512), F32),
        jax.ShapeDtypeStruct((8, 512), F32),
    )
    scratch = [
        vmem(2, 8, 16, 1024),
        vmem(2, 256, 512, dtype=BF16), vmem(2, 256, 512, dtype=BF16),
        vmem(4, 2, 8, 8, 768),
        vmem(512, 768, dtype=BF16), vmem(512, 768, dtype=BF16),
        vmem(3, 256, 128),
        vmem(256, 512, dtype=BF16), vmem(256, 512, dtype=BF16),
        vmem(512, 256, dtype=BF16), vmem(512, 256, dtype=BF16),
        vmem(3, 2, 512, 128),
        vmem(1024, 512, dtype=BF16), vmem(1024, 512, dtype=BF16),
        vmem(128, 512),
        vmem(2, 4, 128, 256), vmem(2, 4, 128, 256), vmem(2, 4, 128, 256),
        vmem(2, 3, 128, 256),
        vmem(2, 128, 256), vmem(2, 128, 256),
        vmem(128, 512), vmem(128, 512), vmem(128, 256),
        vmem(4, 128, 256), vmem(3, 128, 256),
        vmem(4, 128, 128), vmem(3, 128, 128),
        vmem(2, 8, 8, 384), vmem(8, 8, 384),
        vmem(8, 8, 384), vmem(7, 8, 384), vmem(4, 8, 384),
        vmem(2, 8, 16, 1024), vmem(7, 2, 16, 1024),
        vmem(2, 16, 1024), vmem(16, 1024),
        pltpu.SemaphoreType.DMA((COPIES,)), pltpu.SemaphoreType.DMA((COPIES,)),
    ]
    return pl.pallas_call(
        kernel,
        out_shape=outs,
        in_specs=[pl.BlockSpec(memory_space=pltpu.VMEM)] * 6,
        out_specs=(pl.BlockSpec(memory_space=pltpu.VMEM),) * 4,
        scratch_shapes=scratch,
        compiler_params=pltpu.CompilerParams(
            collective_id=0, has_side_effects=True, vmem_limit_bytes=50 * 1024 * 1024),
        name="panel_steps",
    )(x_panels, xbar_panels, bbar_below, l_below, l_cross, dinv)


def solution(mesh):
    in_specs = (
        P(None, "pair"),
        P(None, "pair"),
        P("aux", "pair"),
        P(("aux", "pair"), None),
        P("pair", None),
        P(None, "pair", None),
    )
    out_specs = (P(None, "pair"), P(("aux", "pair"), None), P(None, "pair", None), P("pair", None))
    return jax.shard_map(body, mesh=mesh, in_specs=in_specs, out_specs=out_specs, check_vma=False)
```

time: 1740 us -> 111 us (0.06)
  the two profiles are of different devices: /device:TPU:2 before, /device:TPU:1 now
where the time goes in v1:
time: 111 us
  Pallas kernels  102 us (92%)
  local copies, waits for them, and re-layouts  8.07 us (7%)
    pallas_call x1, Pallas kernels, body(): pl.pallas_call(kernel, out_shape=outs, in_specs=[pl.BlockSpec(memory_spac...  102 us
    unnamed x16, local copies, waits for them, and re-layouts  8.07 us

profile of v1, /device:TPU:1, one launch (start us, length us, event | category | flops | bytes accessed | tf_op | source)
XLA Modules:
  0.0 110.8 jit_solution(6745194977474771320)
XLA Ops:
  0.6 0.0 copy-start
  0.6 1.0 copy-done
  1.7 0.0 copy-start.1
  1.7 1.0 copy-done.1
  2.7 0.0 copy-start.2
  2.7 1.0 copy-done.2
  3.8 0.0 copy-start.3
  3.8 0.8 copy-done.3
  4.6 0.0 copy-start.4
  4.6 0.8 copy-done.4
  5.4 0.0 copy-start.5
  5.4 0.7 copy-done.5
  6.1 102.1 %panel_steps.1 = (f32[1024,128]{1,0:T(8,128)S(1)}, f32[16,1024]{1,0:T(8,128)S(1)}, f32[2,8,512]{2,1,0:T(8,128)S(1)}, f32[8,512]{1,0:T(8,128)S(1)}) custom-call(f32[1024,128]{1,0:T(8,128)S(1)} %copy-done, f32[1024,128]{1,0:T(8,128)S(1)} %copy-done.1, f32[1024,128]{1,0:T(8,128)S(1)} %copy-done.2, f32[16,1024]{1,0:T(8,128)S(1)} %copy-done.3, ...), custom_call_target="tpu_custom_call" | custom-call | tf_op jit(solution)/shard_map/panel_steps/pallas_call | solution.py:336
  108.2 0.8 copy.14
  109.0 0.6 copy.15
  109.6 0.6 copy.16
  110.2 0.6 copy.17
Async XLA Ops:
  0.6 1.0 copy-start
  1.7 1.0 copy-start.1
  2.7 1.0 copy-start.2
  3.8 0.8 copy-start.3
  4.6 0.8 copy-start.4
  5.4 0.7 copy-start.5

commit v2 on v0

v2 whole, which is shorter than its diff:
```python
import jax
import jax.numpy as jnp
from jax import lax
from jax.experimental import pallas as pl
from jax.experimental.pallas import tpu as pltpu
from jax.sharding import PartitionSpec as P

MESH = pl.DeviceIdType.MESH
F32 = jnp.float32
BF16 = jnp.bfloat16
NN = ((1,), (0,))
NT = ((1,), (1,))

CHUNKS = 2
WIDE = 512 // CHUNKS
COPIES = 160
LOADS = 6

Z_ORDER = (1, 7, 2, 6, 3, 5, 4)

STARTS = (0, 384, 896, 1536)
PACKED = 2304


def halves(value):
    high = value.astype(BF16)
    return high, (value - high.astype(F32)).astype(BF16)


def dot3(a, b, dims):
    def one(s, t):
        return lax.dot_general(s, t, (dims, ((), ())), preferred_element_type=F32)

    return one(a[0], b[0]) + (one(a[0], b[1]) + one(a[1], b[0]))


def kernel(
    x_ref, xbar_ref, bbar_ref, l_ref, lc_ref, dinv_ref,
    panels_ref, lbelow_ref, ldiag_ref, lcross_ref,
    x_in, xbar_in, b_in, l_in, lc_in, dinv_in,
    lg, lh, ll, gy, gs, gh, gl, bb, bh, bl, th, tl, xx, xh, xl, xbt,
    cks, csend, crv, yr, accs, accr, pt, ot, ch, ta,
    ds, er, fin, pp, zr, ps, hr,
    ss, rs, ls,
):
    pair = lax.axis_index("pair")
    aux = lax.axis_index("aux")
    y, h, z = pair // 16, (pair // 8) % 2, pair % 8
    lo, core = aux // 2, aux % 2

    def at(dy=0, dh=0, dz=0, dl=0, dcore=0):
        place = ((y + dy) % 4 * 2 + (h + dh) % 2) * 8 + (z + dz) % 8
        return (place, (lo + dl) % 2 * 2 + (core + dcore) % 2)

    started = []
    places = iter(range(COPIES))

    def planned(src, dst, to):
        place = next(places)
        return pltpu.make_async_remote_copy(
            src_ref=src, dst_ref=dst, send_sem=ss.at[place], recv_sem=rs.at[place],
            device_id=to, device_id_type=MESH)

    def keep(src, dst, to):
        copy = planned(src, dst, to)
        copy.start()
        started.append(copy)
        return copy

    def same(ref, to):
        return keep(ref, ref, to)

    my_rows = pl.ds(core * 512, 512)
    loads = []
    for n, (src, dst) in enumerate((
        (l_ref, l_in), (dinv_ref.at[core], dinv_in), (lc_ref, lc_in),
        (bbar_ref.at[pl.ds(y * 256, 256)], b_in), (xbar_ref.at[my_rows], xbar_in), (x_ref, x_in),
    )):
        load = pltpu.make_async_copy(src, dst, ls.at[n])
        load.start()
        loads.append(load)

    barrier = pltpu.get_barrier_semaphore()
    partners = [at(dy=d) for d in (1, 2, 3)] + [at(dl=1), at(dcore=1), at(dl=1, dcore=1)]
    partners += [at(dh=j, dz=k) for j in range(2) for k in range(8) if j or k]
    for partner in partners:
        pl.semaphore_signal(barrier, inc=1, device_id=partner, device_id_type=MESH)

    loads[0].wait()
    for q in range(CHUNKS):
        for side in range(2):
            start = side * 512 + q * WIDE
            lg[q, h, z, side] = l_in[:, start : start + WIDE]
    loads[1].wait()
    loads[2].wait()
    gy[y, :, 0:512] = dinv_in[...]
    gy[y, :, 512:768] = jnp.where(core == 0, lc_in[:, 0:256], lc_in[:, 256:512])

    pl.semaphore_wait(barrier, len(partners))

    l_z, l_h, b_y, g_y, x_y = {}, {}, {}, {}, {}

    def l_first(q):
        mine = lg.at[q, h, z]
        for k in Z_ORDER:
            l_z[q, k] = same(mine, at(dz=k))
        l_h[q, 0] = same(mine, at(dh=1))

    l_first(0)
    for d in (2, 1, 3):
        rows = pl.ds((y + d) % 4 * 256, 256)
        b_y[d] = keep(bbar_ref.at[rows], bb.at[d - 1], at(dy=d))
    for d in (2, 1, 3):
        g_y[d] = same(gy.at[y], at(dy=d))
    for q in range(1, CHUNKS):
        l_first(q)
    for d in (1, 3, 2):
        x_y[d] = keep(x_ref.at[my_rows], xx.at[d - 1, core], at(dy=d))

    def take_b(d, value):
        cols = slice(d * 128, (d + 1) * 128)
        high, low = halves(value)
        bh[:, cols] = high
        bl[:, cols] = low
        high, low = halves(value.T)
        th[cols, :] = high
        tl[cols, :] = low

    loads[3].wait()
    take_b(0, b_in[...])
    loads[4].wait()
    xbt[...] = xbar_in[...].T
    loads[5].wait()
    high, low = halves(x_in[...])
    xh[:, 0:128] = high
    xl[:, 0:128] = low

    def l_forward(q):
        for k in Z_ORDER:
            l_z[q, k].wait_recv()
            l_h[q, k] = same(lg.at[q, h, (z + 8 - k) % 8], at(dh=1))

    l_forward(0)

    for d in (1, 3, 2):
        g_y[d].wait_recv()
    for part in range(4):
        start, width = STARTS[part], (part + 1) * 128
        gs[h, z, :, start : start + width] = gy[part, :, 0:width]
        gs[h, z, :, start + width : start + width + 256] = gy[part, :, 512:768]
    g_z = {k: same(gs.at[h, z], at(dz=k)) for k in Z_ORDER}
    g_h = {0: same(gs.at[h, z], at(dh=1))}

    for d in (1, 3, 2):
        b_y[d].wait_recv()
        take_b(d, bb[d - 1])
    r_c, r_y = {}, {}

    def corr_chunk(q):
        for k in (0,) + Z_ORDER:
            l_h[q, k].wait_recv()
        for side in range(2):
            high, low = halves(lg[q, :, :, side].reshape(256, WIDE))
            lh[q, side] = high
            ll[q, side] = low
        turned = (th[...], tl[...])
        csend[q] = dot3(turned, (lh[q, 1 - core], ll[q, 1 - core]), NN).reshape(4, 128, WIDE)
        r_c[q] = keep(csend.at[q], crv.at[q], at(dcore=1))
        cks[q] = dot3(turned, (lh[q, core], ll[q, core]), NN).reshape(4, 128, WIDE)

    def corr_out(q):
        r_c[q].wait_recv()
        for d in (2, 1, 3, 0):
            cks[q, d] += crv[q, d]
            if d:
                r_y[q, d] = keep(cks.at[q, d], yr.at[q, d - 1], at(dy=4 - d))

    for q in range(CHUNKS):
        if q + 1 < CHUNKS:
            l_forward(q + 1)
        corr_chunk(q)
        corr_out(q)

    x_c = {}
    for d in (1, 3, 2):
        x_y[d].wait_recv()
        x_c[d] = same(xx.at[d - 1, core], at(dcore=1))
    for d in (1, 3, 2):
        x_c[d].wait_recv()
        cols = slice(d * 128, (d + 1) * 128)
        high, low = halves(xx[d - 1].reshape(1024, 128))
        xh[:, cols] = high
        xl[:, cols] = low
    for part in range(4):
        rows = slice(part * 256, (part + 1) * 256)
        product = dot3((bh[...], bl[...]), (xh[rows, :], xl[rows, :]), NT)
        pp[:, :, :, rows] = product.reshape(2, 8, 16, 256)
    f_z = {k: keep(pp.at[:, (z + k) % 8], zr.at[k - 1], at(dz=k)) for k in Z_ORDER}

    r_l = {}

    def corr_last(q):
        for d in (1, 3, 2):
            r_y[q, d].wait_recv()
        accs[q] = (cks[q, 0] + yr[q, 0]) + (yr[q, 1] + yr[q, 2])
        r_l[q] = keep(accs.at[q], accr.at[q], at(dl=1))

    for q in range(CHUNKS - 1):
        corr_last(q)
    for k in Z_ORDER:
        g_z[k].wait_recv()
        g_h[k] = same(gs.at[h, (z + 8 - k) % 8], at(dh=1))
    corr_last(CHUNKS - 1)

    for k in (0,) + Z_ORDER:
        g_h[k].wait_recv()
    for part in range(4):
        start, width = STARTS[part], (part + 1) * 128
        rows = slice(part * 128, width)
        high, low = halves(gs[:, :, :, start : start + width].reshape(128, width))
        gh[rows, 0:width] = high
        gl[rows, 0:width] = low
        if width < 512:
            gh[rows, width:512] = jnp.zeros((128, 512 - width), BF16)
            gl[rows, width:512] = jnp.zeros((128, 512 - width), BF16)
        start += width
        high, low = halves(gs[:, :, :, start : start + 256].reshape(128, 256))
        gh[rows, 512:768] = high
        gl[rows, 512:768] = low
    for q in range(CHUNKS):
        r_l[q].wait_recv()

    def block_of(columns):
        return gh[:, columns], gl[:, columns]

    solve_cols, cross_cols = slice(0, 512), slice(512, 768)
    panel_copy = planned(pt, ot, at(dcore=1))
    cross_copy = planned(ch, ch, at(dcore=1))

    def corrected():
        return xbt[...] - jnp.concatenate([accs[q] + accr[q] for q in range(CHUNKS)], axis=1)

    @pl.when(core == 1)
    def _():
        late = dot3(halves(corrected()), block_of(solve_cols), NN)
        pt[...] = late
        panel_copy.start()
        ch[...] = dot3(halves(late), block_of(cross_cols), NN)
        cross_copy.start()

    @pl.when(core == 0)
    def _():
        rest = corrected()
        panel_copy.wait_recv()
        cross = dot3(halves(ot[...]), block_of(cross_cols), NN)
        cross_copy.wait_recv()
        rest = rest - jnp.concatenate([cross, ch[...]], axis=1)
        pt[...] = dot3(halves(rest), block_of(solve_cols), NN)
        panel_copy.start()

    def lanes(part):
        return pl.ds(pl.multiple_of(part * 128, 128), 128)

    t_y = {d: keep(pt.at[:, lanes((y + d) % 4)], ta.at[d - 1], at(dy=d)) for d in (2, 1, 3)}
    panels_ref[my_rows, :] = pt[...].T
    turned = [pt[:, lanes(y)].T]
    for d in (1, 2, 3):
        t_y[d].wait_recv()
        turned.append(ta[d - 1].T)
    rows = halves(jnp.concatenate(turned, axis=1))

    def x_rows(start):
        where = pl.ds(pl.multiple_of(start, 256), 256)
        return xh[where, :], xl[where, :]

    others = [(j, k) for k in (4, 3, 5, 2, 6, 1, 7, 0) for j in (1, 0) if j or k]

    def spread(cols):
        return [
            planned(ds.at[(h + j) % 2, (z + k) % 8, :, cols], er.at[j * 8 + k, :, cols], at(dh=j, dz=k))
            for j, k in others
        ]

    def total(cols):
        parts = [er[j * 8 + k, :, cols] for j, k in others]
        parts.append(ds[h, z, :, cols])
        while len(parts) > 1:
            parts = [a + b for a, b in zip(parts[::2], parts[1::2])] + parts[len(parts) // 2 * 2 :]
        return -parts[0]

    one, two = slice(0, 256), slice(256, 512)
    ds[:, :, :, one] = dot3(rows, x_rows(core * 512 + lo * 256), NT).reshape(2, 8, 8, 256)
    d_one, d_two = spread(one), spread(two)
    for copy in d_one:
        copy.start()
    started.extend(d_one)

    @pl.when(core == 1)
    def _():
        ds[:, :, :, two] = dot3(rows, x_rows(lo * 256), NT).reshape(2, 8, 8, 256)
        for copy in d_two:
            copy.start()

    for k in Z_ORDER:
        f_z[k].wait_recv()
    sums = pp[:, z]
    for k in range(7):
        sums = sums + zr[k]
    ps[...] = sums
    f_h = keep(ps.at[1 - h], hr, at(dh=1))

    @pl.when(core == 1)
    def _():
        for copy in d_two:
            copy.wait()
        fin[aux, :, two] = total(two)

    @pl.when(core == 0)
    def _():
        fin[aux, :, two] = jnp.zeros((8, 256), F32)

    for copy in d_one:
        copy.wait_recv()
    fin[aux, :, one] = total(one)
    d_a = [same(fin.at[aux], at(dl=j // 2, dcore=j % 2)) for j in (1, 2, 3)]

    panel_copy.wait_send()

    @pl.when(core == 1)
    def _():
        cross_copy.wait_send()
        panel_copy.wait_recv()

    panels_ref[pl.ds((1 - core) * 512, 512), :] = ot[...].T
    f_h.wait_recv()
    lbelow_ref[...] = -(ps[h] + hr[...])
    for copy in d_a:
        copy.wait_recv()
    for side in range(2):
        cols = slice(side * 256, (side + 1) * 256)
        for which in range(2):
            ldiag_ref[which, :, cols] = fin[side * 2 + which, :, one]
        lcross_ref[:, cols] = fin[side * 2 + 1, :, two]

    for copy in started:
        copy.wait_send()


def body(x_panels, xbar_panels, bbar_below, l_below, l_cross, dinv):
    def vmem(*shape, dtype=F32):
        return pltpu.VMEM(shape, dtype)

    outs = (
        jax.ShapeDtypeStruct((1024, 128), F32),
        jax.ShapeDtypeStruct((16, 1024), F32),
        jax.ShapeDtypeStruct((2, 8, 512), F32),
        jax.ShapeDtypeStruct((8, 512), F32),
    )
    scratch = [
        vmem(1024, 128), vmem(512, 128), vmem(256, 128),
        vmem(16, 1024), vmem(8, 512), vmem(8, 512),
        vmem(CHUNKS, 2, 8, 2, 16, WIDE),
        vmem(CHUNKS, 2, 256, WIDE, dtype=BF16), vmem(CHUNKS, 2, 256, WIDE, dtype=BF16),
        vmem(4, 8, 768), vmem(2, 8, 8, PACKED),
        vmem(512, 768, dtype=BF16), vmem(512, 768, dtype=BF16),
        vmem(3, 256, 128),
        vmem(256, 512, dtype=BF16), vmem(256, 512, dtype=BF16),
        vmem(512, 256, dtype=BF16), vmem(512, 256, dtype=BF16),
        vmem(3, 2, 512, 128),
        vmem(1024, 512, dtype=BF16), vmem(1024, 512, dtype=BF16),
        vmem(128, 512),
        vmem(CHUNKS, 4, 128, WIDE), vmem(CHUNKS, 4, 128, WIDE),
        vmem(CHUNKS, 4, 128, WIDE), vmem(CHUNKS, 3, 128, WIDE),
        vmem(CHUNKS, 128, WIDE), vmem(CHUNKS, 128, WIDE),
        vmem(128, 512), vmem(128, 512), vmem(128, 256), vmem(3, 128, 128),
        vmem(2, 8, 8, 512), vmem(16, 8, 512), vmem(4, 8, 512),
        vmem(2, 8, 16, 1024), vmem(7, 2, 16, 1024),
        vmem(2, 16, 1024), vmem(16, 1024),
        pltpu.SemaphoreType.DMA((COPIES,)), pltpu.SemaphoreType.DMA((COPIES,)),
        pltpu.SemaphoreType.DMA((LOADS,)),
    ]
    return pl.pallas_call(
        kernel,
        out_shape=outs,
        in_specs=[pl.BlockSpec(memory_space=pltpu.MemorySpace.HBM)] * 6,
        out_specs=(pl.BlockSpec(memory_space=pltpu.VMEM),) * 4,
        scratch_shapes=scratch,
        compiler_params=pltpu.CompilerParams(
            collective_id=0, has_side_effects=True, vmem_limit_bytes=60 * 1024 * 1024),
        name="panel_steps",
    )(x_panels, xbar_panels, bbar_below, l_below, l_cross, dinv)


def solution(mesh):
    in_specs = (
        P(None, "pair"),
        P(None, "pair"),
        P("aux", "pair"),
        P(("aux", "pair"), None),
        P("pair", None),
        P(None, "pair", None),
    )
    out_specs = (P(None, "pair"), P(("aux", "pair"), None), P(None, "pair", None), P("pair", None))
    return jax.shard_map(body, mesh=mesh, in_specs=in_specs, out_specs=out_specs, check_vma=False)
```

time: 1740 us -> 80.6 us (0.05)
  the two profiles are of different devices: /device:TPU:2 before, /device:TPU:1 now
where the time goes in v2:
time: 80.6 us; the launch traced here: 80.3 us
  Pallas kernels  75.7 us (94%)
  local copies, waits for them, and re-layouts  4 us (5%)
    pallas_call x1, Pallas kernels, body(): pl.pallas_call(kernel, out_shape=outs, in_specs=[pl.BlockSpec(memory_spac...  75.7 us
    unnamed x10, local copies, waits for them, and re-layouts  4 us

profile of v2, /device:TPU:1, one launch (start us, length us, event | category | flops | bytes accessed | tf_op | source)
XLA Modules:
  0.0 80.3 jit_solution(17790905009948251066)
XLA Ops:
  0.6 75.7 %panel_steps.1 = (f32[1024,128]{1,0:T(8,128)}, f32[16,1024]{1,0:T(8,128)}, f32[2,8,512]{2,1,0:T(8,128)}, f32[8,512]{1,0:T(8,128)}) custom-call(f32[1024,128]{1,0:T(8,128)} %x_ref.1, f32[1024,128]{1,0:T(8,128)} %xbar_ref.1, f32[1024,128]{1,0:T(8,128)} %bbar_ref.1, f32[16,1024]{1,0:T(8,128)} %l_ref.1, f32[8,512]{1,0:T(8,128)} %lc_ref.1, f32[2,8,512]{2,1,0:T(8,128)} %dinv_ref.1), custom_call_target="tpu_custom_call" | custom-call | tf_op jit(solution)/shard_map/panel_steps/pallas_call | solution.py:382
  76.3 0.0 copy-start
  76.3 1.9 %copy.14 = f32[1024,128]{1,0:T(8,128)} copy(f32[1024,128]{1,0:T(8,128)} %get-tuple-element.8) | data formatting | bytes 1048576
  78.2 0.0 copy-done
  78.2 0.0 copy-start.1
  78.2 0.6 copy.15
  78.9 0.1 copy-done.1
  79.0 0.0 copy-start.2
  79.0 0.6 copy.16
  79.6 0.1 copy-done.2
  79.7 0.6 copy.17
Async XLA Ops:
  76.3 1.9 %copy-start = (f32[16,1024]{1,0:T(8,128)S(1)}, f32[16,1024]{1,0:T(8,128)}, u32[]{:S(2)}) copy-start(f32[16,1024]{1,0:T(8,128)} %get-tuple-element.9) | copy-start | bytes 196612
  78.2 0.8 copy-start.1
  79.0 0.7 copy-start.2

commit v3 on v2

--- a/solution.py
+++ b/solution.py
@@ -11,10 +11,14 @@
 NN = ((1,), (0,))
 NT = ((1,), (1,))
 
-CHUNKS = 2
+CHUNKS = 4
 WIDE = 512 // CHUNKS
-COPIES = 160
+COPIES = 200
 LOADS = 6
+
+G_START = 0
+BELOW_AT = 3
+G_TURNS = ((), (), (1, 7, 2), (6, 3, 5, 4))
 
 Z_ORDER = (1, 7, 2, 6, 3, 5, 4)
 
@@ -40,7 +44,7 @@
     x_in, xbar_in, b_in, l_in, lc_in, dinv_in,
     lg, lh, ll, gy, gs, gh, gl, bb, bh, bl, th, tl, xx, xh, xl, xbt,
     cks, csend, crv, yr, accs, accr, pt, ot, ch, ta,
-    ds, er, fin, pp, zr, ps, hr,
+    ds, er, fin, pp, pb, zr, ps, hr, hh, ph, zh,
     ss, rs, ls,
 ):
     pair = lax.axis_index("pair")
@@ -82,7 +86,7 @@
 
     barrier = pltpu.get_barrier_semaphore()
     partners = [at(dy=d) for d in (1, 2, 3)] + [at(dl=1), at(dcore=1), at(dl=1, dcore=1)]
-    partners += [at(dh=j, dz=k) for j in range(2) for k in range(8) if j or k]
+    partners += [at(dz=k) for k in range(1, 8)] + [at(dh=1)]
     for partner in partners:
         pl.semaphore_signal(barrier, inc=1, device_id=partner, device_id_type=MESH)
 
@@ -142,14 +146,27 @@
 
     l_forward(0)
 
-    for d in (1, 3, 2):
-        g_y[d].wait_recv()
-    for part in range(4):
-        start, width = STARTS[part], (part + 1) * 128
-        gs[h, z, :, start : start + width] = gy[part, :, 0:width]
-        gs[h, z, :, start + width : start + width + 256] = gy[part, :, 512:768]
-    g_z = {k: same(gs.at[h, z], at(dz=k)) for k in Z_ORDER}
-    g_h = {0: same(gs.at[h, z], at(dh=1))}
+    g_z, g_h = {}, {}
+
+    def g_pack():
+        for d in (1, 3, 2):
+            g_y[d].wait_recv()
+        for part in range(4):
+            start, width = STARTS[part], (part + 1) * 128
+            gs[h, z, :, start : start + width] = gy[part, :, 0:width]
+            gs[h, z, :, start + width : start + width + 256] = gy[part, :, 512:768]
+
+    def g_first():
+        for k in Z_ORDER:
+            g_z[k] = same(gs.at[h, z], at(dz=k))
+        g_h[0] = same(gs.at[h, z], at(dh=1))
+
+    def g_forward(some):
+        for k in some:
+            g_z[k].wait_recv()
+            g_h[k] = same(gs.at[h, (z + 8 - k) % 8], at(dh=1))
+
+    g_pack()
 
     for d in (1, 3, 2):
         b_y[d].wait_recv()
@@ -175,27 +192,45 @@
             if d:
                 r_y[q, d] = keep(cks.at[q, d], yr.at[q, d - 1], at(dy=4 - d))
 
+    x_c, f_z, f_h = {}, {}, {}
+
+    def below_products():
+        for d in (1, 3, 2):
+            x_y[d].wait_recv()
+            x_c[d] = same(xx.at[d - 1, core], at(dcore=1))
+        for d in (1, 3, 2):
+            x_c[d].wait_recv()
+            cols = slice(d * 128, (d + 1) * 128)
+            high, low = halves(xx[d - 1].reshape(1024, 128))
+            xh[:, cols] = high
+            xl[:, cols] = low
+        for part in range(4):
+            rows = slice(part * 256, (part + 1) * 256)
+            product = dot3((bh[...], bl[...]), (xh[rows, :], xl[rows, :]), NT)
+            product = product.reshape(2, 8, 16, 256)
+            if part < 3:
+                pp[:, :, :, rows] = product
+            else:
+                pb[...] = product
+        for k in Z_ORDER:
+            f_z[0, k] = keep(pp.at[:, (z + k) % 8], zr.at[k - 1], at(dz=k))
+
+    def below_second():
+        f_h[1].wait_recv()
+        ph[...] = pb[h] + hh[...]
+        for k in Z_ORDER:
+            f_z[1, k] = keep(ph.at[(z + k) % 8], zh.at[k - 1], at(dz=k))
+
     for q in range(CHUNKS):
         if q + 1 < CHUNKS:
             l_forward(q + 1)
+        if q == G_START:
+            g_first()
         corr_chunk(q)
         corr_out(q)
-
-    x_c = {}
-    for d in (1, 3, 2):
-        x_y[d].wait_recv()
-        x_c[d] = same(xx.at[d - 1, core], at(dcore=1))
-    for d in (1, 3, 2):
-        x_c[d].wait_recv()
-        cols = slice(d * 128, (d + 1) * 128)
-        high, low = halves(xx[d - 1].reshape(1024, 128))
-        xh[:, cols] = high
-        xl[:, cols] = low
-    for part in range(4):
-        rows = slice(part * 256, (part + 1) * 256)
-        product = dot3((bh[...], bl[...]), (xh[rows, :], xl[rows, :]), NT)
-        pp[:, :, :, rows] = product.reshape(2, 8, 16, 256)
-    f_z = {k: keep(pp.at[:, (z + k) % 8], zr.at[k - 1], at(dz=k)) for k in Z_ORDER}
+        g_forward(G_TURNS[q])
+        if q == BELOW_AT:
+            below_products()
 
     r_l = {}
 
@@ -205,12 +240,8 @@
         accs[q] = (cks[q, 0] + yr[q, 0]) + (yr[q, 1] + yr[q, 2])
         r_l[q] = keep(accs.at[q], accr.at[q], at(dl=1))
 
-    for q in range(CHUNKS - 1):
+    for q in range(CHUNKS):
         corr_last(q)
-    for k in Z_ORDER:
-        g_z[k].wait_recv()
-        g_h[k] = same(gs.at[h, (z + 8 - k) % 8], at(dh=1))
-    corr_last(CHUNKS - 1)
 
     for k in (0,) + Z_ORDER:
         g_h[k].wait_recv()
@@ -229,6 +260,7 @@
         gl[rows, 512:768] = low
     for q in range(CHUNKS):
         r_l[q].wait_recv()
+    f_h[1] = keep(pb.at[1 - h], hh, at(dh=1))
 
     def block_of(columns):
         return gh[:, columns], gl[:, columns]
@@ -301,13 +333,14 @@
         for copy in d_two:
             copy.start()
 
+    below_second()
     for k in Z_ORDER:
-        f_z[k].wait_recv()
+        f_z[0, k].wait_recv()
     sums = pp[:, z]
     for k in range(7):
         sums = sums + zr[k]
     ps[...] = sums
-    f_h = keep(ps.at[1 - h], hr, at(dh=1))
+    f_h[0] = keep(ps.at[1 - h], hr, at(dh=1))
 
     @pl.when(core == 1)
     def _():
@@ -332,8 +365,14 @@
         panel_copy.wait_recv()
 
     panels_ref[pl.ds((1 - core) * 512, 512), :] = ot[...].T
-    f_h.wait_recv()
-    lbelow_ref[...] = -(ps[h] + hr[...])
+    for k in Z_ORDER:
+        f_z[1, k].wait_recv()
+    sums = ph[z]
+    for k in range(7):
+        sums = sums + zh[k]
+    lbelow_ref[:, 768:1024] = -sums
+    f_h[0].wait_recv()
+    lbelow_ref[:, 0:768] = -(ps[h] + hr[...])
     for copy in d_a:
         copy.wait_recv()
     for side in range(2):
@@ -374,8 +413,9 @@
         vmem(CHUNKS, 128, WIDE), vmem(CHUNKS, 128, WIDE),
         vmem(128, 512), vmem(128, 512), vmem(128, 256), vmem(3, 128, 128),
         vmem(2, 8, 8, 512), vmem(16, 8, 512), vmem(4, 8, 512),
-        vmem(2, 8, 16, 1024), vmem(7, 2, 16, 1024),
-        vmem(2, 16, 1024), vmem(16, 1024),
+        vmem(2, 8, 16, 768), vmem(2, 8, 16, 256), vmem(7, 2, 16, 768),
+        vmem(2, 16, 768), vmem(16, 768),
+        vmem(8, 16, 256), vmem(8, 16, 256), vmem(7, 16, 256),
         pltpu.SemaphoreType.DMA((COPIES,)), pltpu.SemaphoreType.DMA((COPIES,)),
         pltpu.SemaphoreType.DMA((LOADS,)),
     ]

time: 80.6 us -> 76.5 us (0.949)
  Pallas kernels: 75.7 us -> 71.6 us
    pallas_call x1, Pallas kernels: 75.7 us -> 71.6 us  [body(): pl.pallas_call(kernel, out_shape=outs, in_specs=[pl.BlockSpec(memory_spac...]
where the time goes in v3:
time: 76.5 us; the launch traced here: 76.2 us
  Pallas kernels  71.6 us (94%)
  local copies, waits for them, and re-layouts  4 us (5%)
    pallas_call x1, Pallas kernels, body(): pl.pallas_call(kernel, out_shape=outs, in_specs=[pl.BlockSpec(memory_spac...  71.6 us
    unnamed x10, local copies, waits for them, and re-layouts  4 us

profile of v3, /device:TPU:1, one launch (start us, length us, event | category | flops | bytes accessed | tf_op | source)
XLA Modules:
  0.0 76.2 jit_solution(12676780431401779263)
XLA Ops:
  0.6 71.6 %panel_steps.1 = (f32[1024,128]{1,0:T(8,128)}, f32[16,1024]{1,0:T(8,128)}, f32[2,8,512]{2,1,0:T(8,128)}, f32[8,512]{1,0:T(8,128)}) custom-call(f32[1024,128]{1,0:T(8,128)} %x_ref.1, f32[1024,128]{1,0:T(8,128)} %xbar_ref.1, f32[1024,128]{1,0:T(8,128)} %bbar_ref.1, f32[16,1024]{1,0:T(8,128)} %l_ref.1, f32[8,512]{1,0:T(8,128)} %lc_ref.1, f32[2,8,512]{2,1,0:T(8,128)} %dinv_ref.1), custom_call_target="tpu_custom_call" | custom-call | tf_op jit(solution)/shard_map/panel_steps/pallas_call | solution.py:422
  72.2 0.0 copy-start
  72.2 1.9 %copy.14 = f32[1024,128]{1,0:T(8,128)} copy(f32[1024,128]{1,0:T(8,128)} %get-tuple-element.8) | data formatting | bytes 1048576
  74.1 0.0 copy-done
  74.1 0.0 copy-start.1
  74.1 0.6 copy.15
  74.8 0.1 copy-done.1
  74.9 0.0 copy-start.2
  74.9 0.6 copy.16
  75.5 0.1 copy-done.2
  75.6 0.6 copy.17
Async XLA Ops:
  72.2 1.9 %copy-start = (f32[16,1024]{1,0:T(8,128)S(1)}, f32[16,1024]{1,0:T(8,128)}, u32[]{:S(2)}) copy-start(f32[16,1024]{1,0:T(8,128)} %get-tuple-element.9) | copy-start | bytes 196612
  74.1 0.8 copy-start.1
  74.9 0.7 copy-start.2

commit v4 on v3

--- a/solution.py
+++ b/solution.py
@@ -208,10 +208,10 @@
             rows = slice(part * 256, (part + 1) * 256)
             product = dot3((bh[...], bl[...]), (xh[rows, :], xl[rows, :]), NT)
             product = product.reshape(2, 8, 16, 256)
-            if part < 3:
+            if part < 2:
                 pp[:, :, :, rows] = product
             else:
-                pb[...] = product
+                pb[:, :, :, part % 2 * 256 : part % 2 * 256 + 256] = product
         for k in Z_ORDER:
             f_z[0, k] = keep(pp.at[:, (z + k) % 8], zr.at[k - 1], at(dz=k))
 
@@ -370,9 +370,9 @@
     sums = ph[z]
     for k in range(7):
         sums = sums + zh[k]
-    lbelow_ref[:, 768:1024] = -sums
+    lbelow_ref[:, 512:1024] = -sums
     f_h[0].wait_recv()
-    lbelow_ref[:, 0:768] = -(ps[h] + hr[...])
+    lbelow_ref[:, 0:512] = -(ps[h] + hr[...])
     for copy in d_a:
         copy.wait_recv()
     for side in range(2):
@@ -413,9 +413,9 @@
         vmem(CHUNKS, 128, WIDE), vmem(CHUNKS, 128, WIDE),
         vmem(128, 512), vmem(128, 512), vmem(128, 256), vmem(3, 128, 128),
         vmem(2, 8, 8, 512), vmem(16, 8, 512), vmem(4, 8, 512),
-        vmem(2, 8, 16, 768), vmem(2, 8, 16, 256), vmem(7, 2, 16, 768),
-        vmem(2, 16, 768), vmem(16, 768),
-        vmem(8, 16, 256), vmem(8, 16, 256), vmem(7, 16, 256),
+        vmem(2, 8, 16, 512), vmem(2, 8, 16, 512), vmem(7, 2, 16, 512),
+        vmem(2, 16, 512), vmem(16, 512),
+        vmem(8, 16, 512), vmem(8, 16, 512), vmem(7, 16, 512),
         pltpu.SemaphoreType.DMA((COPIES,)), pltpu.SemaphoreType.DMA((COPIES,)),
         pltpu.SemaphoreType.DMA((LOADS,)),
     ]

time: 76.5 us -> 75.4 us (0.986)
  Pallas kernels: 71.6 us -> 70.5 us
    pallas_call x1, Pallas kernels: 71.6 us -> 70.5 us  [body(): pl.pallas_call(kernel, out_shape=outs, in_specs=[pl.BlockSpec(memory_spac...]
where the time goes in v4:
time: 75.4 us; the launch traced here: 75.1 us
  Pallas kernels  70.5 us (94%)
  local copies, waits for them, and re-layouts  4 us (5%)
    pallas_call x1, Pallas kernels, body(): pl.pallas_call(kernel, out_shape=outs, in_specs=[pl.BlockSpec(memory_spac...  70.5 us
    unnamed x10, local copies, waits for them, and re-layouts  4 us

profile of v4, /device:TPU:1, one launch (start us, length us, event | category | flops | bytes accessed | tf_op | source)
XLA Modules:
  0.0 75.1 jit_solution(3269709812573800668)
XLA Ops:
  0.6 70.5 %panel_steps.1 = (f32[1024,128]{1,0:T(8,128)}, f32[16,1024]{1,0:T(8,128)}, f32[2,8,512]{2,1,0:T(8,128)}, f32[8,512]{1,0:T(8,128)}) custom-call(f32[1024,128]{1,0:T(8,128)} %x_ref.1, f32[1024,128]{1,0:T(8,128)} %xbar_ref.1, f32[1024,128]{1,0:T(8,128)} %bbar_ref.1, f32[16,1024]{1,0:T(8,128)} %l_ref.1, f32[8,512]{1,0:T(8,128)} %lc_ref.1, f32[2,8,512]{2,1,0:T(8,128)} %dinv_ref.1), custom_call_target="tpu_custom_call" | custom-call | tf_op jit(solution)/shard_map/panel_steps/pallas_call | solution.py:422
  71.1 0.0 copy-start
  71.1 1.9 %copy.14 = f32[1024,128]{1,0:T(8,128)} copy(f32[1024,128]{1,0:T(8,128)} %get-tuple-element.8) | data formatting | bytes 1048576
  73.0 0.0 copy-done
  73.0 0.0 copy-start.1
  73.0 0.6 copy.15
  73.7 0.1 copy-done.1
  73.8 0.0 copy-start.2
  73.8 0.6 copy.16
  74.4 0.1 copy-done.2
  74.5 0.6 copy.17
Async XLA Ops:
  71.1 1.9 %copy-start = (f32[16,1024]{1,0:T(8,128)S(1)}, f32[16,1024]{1,0:T(8,128)}, u32[]{:S(2)}) copy-start(f32[16,1024]{1,0:T(8,128)} %get-tuple-element.9) | copy-start | bytes 196612
  73.0 0.8 %copy-start.1 = (f32[2,8,512]{2,1,0:T(8,128)S(1)}, f32[2,8,512]{2,1,0:T(8,128)}, u32[]{:S(2)}) copy-start(f32[2,8,512]{2,1,0:T(8,128)} %get-tuple-element.10) | copy-start | bytes 98308
  73.8 0.7 copy-start.2

commit v5 on v4

--- a/solution.py
+++ b/solution.py
@@ -85,7 +85,7 @@
         loads.append(load)
 
     barrier = pltpu.get_barrier_semaphore()
-    partners = [at(dy=d) for d in (1, 2, 3)] + [at(dl=1), at(dcore=1), at(dl=1, dcore=1)]
+    partners = [at(dy=d) for d in (1, 2, 3)] + [at(dl=1), at(dcore=1)]
     partners += [at(dz=k) for k in range(1, 8)] + [at(dh=1)]
     for partner in partners:
         pl.semaphore_signal(barrier, inc=1, device_id=partner, device_id_type=MESH)
@@ -242,6 +242,7 @@
 
     for q in range(CHUNKS):
         corr_last(q)
+    f_h[1] = keep(pb.at[1 - h], hh, at(dh=1))
 
     for k in (0,) + Z_ORDER:
         g_h[k].wait_recv()
@@ -260,7 +261,6 @@
         gl[rows, 512:768] = low
     for q in range(CHUNKS):
         r_l[q].wait_recv()
-    f_h[1] = keep(pb.at[1 - h], hh, at(dh=1))
 
     def block_of(columns):
         return gh[:, columns], gl[:, columns]

time: 75.4 us -> 75.6 us (level)
  no operation moved by 1% of the time
where the time goes in v5:
time: 75.6 us; the launch traced here: 75.4 us
  Pallas kernels  70.8 us (94%)
  local copies, waits for them, and re-layouts  4 us (5%)
    pallas_call x1, Pallas kernels, body(): pl.pallas_call(kernel, out_shape=outs, in_specs=[pl.BlockSpec(memory_spac...  70.8 us
    unnamed x10, local copies, waits for them, and re-layouts  4 us

profile of v5, /device:TPU:1, one launch (start us, length us, event | category | flops | bytes accessed | tf_op | source)
XLA Modules:
  0.0 75.4 jit_solution(7587280172800223296)
XLA Ops:
  0.6 70.8 %panel_steps.1 = (f32[1024,128]{1,0:T(8,128)}, f32[16,1024]{1,0:T(8,128)}, f32[2,8,512]{2,1,0:T(8,128)}, f32[8,512]{1,0:T(8,128)}) custom-call(f32[1024,128]{1,0:T(8,128)} %x_ref.1, f32[1024,128]{1,0:T(8,128)} %xbar_ref.1, f32[1024,128]{1,0:T(8,128)} %bbar_ref.1, f32[16,1024]{1,0:T(8,128)} %l_ref.1, f32[8,512]{1,0:T(8,128)} %lc_ref.1, f32[2,8,512]{2,1,0:T(8,128)} %dinv_ref.1), custom_call_target="tpu_custom_call" | custom-call | tf_op jit(solution)/shard_map/panel_steps/pallas_call | solution.py:422
  71.4 0.0 copy-start
  71.4 1.9 %copy.14 = f32[1024,128]{1,0:T(8,128)} copy(f32[1024,128]{1,0:T(8,128)} %get-tuple-element.8) | data formatting | bytes 1048576
  73.3 0.0 copy-done
  73.3 0.0 copy-start.1
  73.3 0.6 copy.15
  73.9 0.1 copy-done.1
  74.1 0.0 copy-start.2
  74.1 0.6 copy.16
  74.7 0.1 copy-done.2
  74.8 0.6 copy.17
Async XLA Ops:
  71.4 1.9 %copy-start = (f32[16,1024]{1,0:T(8,128)S(1)}, f32[16,1024]{1,0:T(8,128)}, u32[]{:S(2)}) copy-start(f32[16,1024]{1,0:T(8,128)} %get-tuple-element.9) | copy-start | bytes 196612
  73.3 0.8 %copy-start.1 = (f32[2,8,512]{2,1,0:T(8,128)S(1)}, f32[2,8,512]{2,1,0:T(8,128)}, u32[]{:S(2)}) copy-start(f32[2,8,512]{2,1,0:T(8,128)} %get-tuple-element.10) | copy-start | bytes 98308
  74.1 0.7 copy-start.2
